TPU v7x, 32 devices: a whole 2x2x4 slice. The times are simulated.
32 devices in a mesh: section: 4 (over z), expert: 8 (over y, x, core).
Axes of the slice: x: 2, y: 2, z: 4, core: 2. Of those that a mesh axis runs over, the one named last changes fastest.
Arguments:
- tokens: bfloat16 [8, 64, 2048], P(None, 'expert', 'section'), may hold values from -6 to 6
- norm_gain: float32 [4, 2048], P('section'), may hold values from 0.1 to 1.9
- gate_weight: bfloat16 [4, 32, 2048, 384], P('section', 'expert'), may hold values from -0.125 to 0.125
- up_weight: bfloat16 [4, 32, 2048, 384], P('section', 'expert'), may hold values from -0.125 to 0.125
- down_weight: bfloat16 [4, 32, 384, 2048], P('section', 'expert'), may hold values from -0.3125 to 0.3125
- expert_ids: int32 [4, 8, 64, 8], P('section', None, 'expert'), may hold values from 0 to 31, all different within a row; in each aligned block of 8 rows (0 to 7, 8 to 15, ..., all dimensions but the last counted through in order) at most 2 rows name the same one
- gate_probs: float32 [4, 8, 64, 8], P('section', None, 'expert'), may hold values from 0.05 to 1
Outputs:
- hidden_states: bfloat16 [4, 8, 64, 2048], P('section', None, 'expert')
Inputs may be any that keep to these rules, and one draw needn't show every extreme that they name: `expert_ids`: in the 8 rows of one index of expert for one layer and micro-batch (aligned blocks of 8 rows), no expert is named by more than 2 rows, a bound that some block reaches in every draw.
All inputs are finite; a program needn't handle non-finite values.
Results may differ from a plain program's by a relative error of at most 0.04.
Values may be sent and summed in bfloat16 or wider, within the bound.
A program may use at most 64 MiB of HBM per device.

v0:
```python
import jax
import jax.numpy as jnp
from jax import lax
from jax.sharding import PartitionSpec as P

CAP = 2


EPS = 1e-06


def passed_along(value, axis, by):
    length = lax.axis_size(axis)
    pairs = [(i, i + by) for i in range(length) if 0 <= i + by < length]
    return lax.ppermute(value, axis, pairs)


def expert_block(routed, w_gate, w_up, w_down):
    gate_proj = jnp.einsum("escd,edf->escf", routed, w_gate, preferred_element_type=jnp.float32)
    up_proj = jnp.einsum("escd,edf->escf", routed, w_up, preferred_element_type=jnp.float32)
    active = (jax.nn.silu(gate_proj) * up_proj).astype(jnp.bfloat16)
    return jnp.einsum("escf,efd->escd", active, w_down, preferred_element_type=jnp.float32).astype(
        jnp.bfloat16
    )


def slot_numbers(flat_ids, experts, capacity):
    onehot = (flat_ids[..., None] == jnp.arange(experts, dtype=jnp.int32)).astype(jnp.int32)
    before = jnp.cumsum(onehot, axis=-2) - onehot
    return flat_ids * capacity + jnp.sum(onehot * before, axis=-1)


def moe_layer(layer_input, norm_scale, expert_list, gate_share, w_gate, w_up, w_down):
    row_count, columns = layer_input.shape
    top_count = expert_list.shape[1]
    experts_local = w_gate.shape[0]
    groups = lax.axis_size("expert")
    experts = experts_local * groups
    capacity = CAP
    widened = layer_input.astype(jnp.float32)
    normed = (
        widened * lax.rsqrt(jnp.mean(widened * widened, axis=-1, keepdims=True) + EPS) * norm_scale
    ).astype(jnp.bfloat16)
    weight = gate_share / jnp.sum(gate_share, axis=-1, keepdims=True)
    slot_index = slot_numbers(
        expert_list.reshape(row_count * top_count), experts, capacity
    ).reshape(row_count, top_count)
    target = jnp.arange(experts * capacity, dtype=jnp.int32)
    placement = jnp.sum(
        (slot_index[None, :, :] == target[:, None, None]).astype(jnp.bfloat16), axis=2
    )
    sending = jnp.dot(placement, normed, preferred_element_type=jnp.float32).astype(jnp.bfloat16)
    sending = sending.reshape(experts, 1, capacity, columns)
    results = expert_block(
        lax.all_to_all(sending, "expert", split_axis=0, concat_axis=1, tiled=True),
        w_gate,
        w_up,
        w_down,
    )
    returned = lax.all_to_all(results, "expert", split_axis=1, concat_axis=0, tiled=True)
    returns_wide = returned.reshape(experts * capacity, columns).astype(jnp.float32)
    mixing = jnp.sum(
        (slot_index[:, :, None] == target[None, None, :]).astype(jnp.float32) * weight[:, :, None],
        axis=1,
    )
    mixed = jnp.dot(mixing, returns_wide, precision=lax.Precision.HIGHEST)
    return (widened + mixed).astype(jnp.bfloat16)


def local(tokens, norm_gain, gate_weight, up_weight, down_weight, expert_ids, gate_probs):
    section_index = lax.axis_index("section")
    section_count = lax.axis_size("section")
    full_tokens = lax.all_gather(tokens, "section", axis=2, tiled=True)
    micro_count, row_count, columns = full_tokens.shape
    turn_count = section_count + micro_count - 1
    norm_scale = norm_gain[0]
    w_gate = gate_weight[0]
    w_up = up_weight[0]
    w_down = down_weight[0]
    layer_ids = expert_ids[0]
    layer_probs = gate_probs[0]

    def advance(turn_index, state_pair):
        incoming, hidden_out = state_pair
        micro_index = turn_index - section_index
        is_valid = (micro_index >= 0) & (micro_index < micro_count)
        micro_pick = jnp.clip(micro_index, 0, micro_count - 1)
        fresh_rows = lax.dynamic_index_in_dim(full_tokens, micro_pick, 0, keepdims=False)
        layer_input = jnp.where(section_index == 0, fresh_rows, incoming)
        expert_list = lax.dynamic_index_in_dim(layer_ids, micro_pick, 0, keepdims=False)
        gate_share = lax.dynamic_index_in_dim(layer_probs, micro_pick, 0, keepdims=False)
        layer_output = moe_layer(
            layer_input, norm_scale, expert_list, gate_share, w_gate, w_up, w_down
        )
        updated = lax.dynamic_update_index_in_dim(hidden_out, layer_output, micro_pick, 0)
        hidden_out = jnp.where(is_valid, updated, hidden_out)
        passed = passed_along(layer_output, "section", 1)
        return (passed, hidden_out)

    initial = (
        jnp.zeros((row_count, columns), jnp.bfloat16),
        jnp.zeros((micro_count, row_count, columns), jnp.bfloat16),
    )
    final_pair = lax.fori_loop(0, turn_count, advance, initial)
    return final_pair[1][None]


def solution(mesh):
    in_specs = (
        P(None, "expert", "section"),
        P("section", None),
        P("section", "expert", None, None),
        P("section", "expert", None, None),
        P("section", "expert", None, None),
        P("section", None, "expert", None),
        P("section", None, "expert", None),
    )
    out_specs = P("section", None, "expert", None)
    return jax.shard_map(local, mesh=mesh, in_specs=in_specs, out_specs=out_specs, check_vma=False)
```

profile of v0, /device:TPU:24, one launch (start us, length us, event | category | flops | bytes accessed | tf_op | source)
XLA Modules:
  0.0 476.5 jit_solution(16912659631257964686)
XLA Ops:
  0.0 14.7 %all_gather.3 = bf16[8,8,2048]{2,1,0:T(8,128)(2,1)S(1)} all-gather(bf16[8,8,512]{2,1,0:T(8,128)(2,1)} %param.9), channel_id=1, replica_groups=mesh['section'=4,'expert'=8] {'section'}, dimensions={2}, use_global_device_ids=true | all-gather | bytes 327680 | tf_op jit(solution)/shard_map/all_gather | solution.py:73
  14.7 461.1 %while.17 = (s32[]{:T(128)}, bf16[8,2048]{1,0:T(8,128)(2,1)S(1)}, bf16[8,8,2048]{2,1,0:T(8,128)(2,1)S(1)}, pred[]{:T(512)}, s32[]{:T(128)}, /*index=5*/bf16[8,8,...) while((s32[]{:T(128)}, bf16[8,2048]{1,0:T(8,128)(2,1)S(1)}, ...), condition=%wide.region_7.8_spmd, body=%wide.region_0.7_spmd.sunk | while | flops 317443392 | bytes 23976216 | solution.py:104
  24.1 5.4 %all-to-all-done = bf16[32,1,2,2048]{3,2,1,0:T(2,128)(2,1)S(1)} async-done(((bf16[32,1,2,2048]{3,2,1,0:T(2,128)(2,1)}), bf16[32,1,2,2048]{3,2,1,0:T(2,128)(2,1)S(1)}, u32[]{:S(2)}, u32[]{:S(2)}) %all-to-all-start) | async-done | bytes 262176 | tf_op jit(solution)/shard_map/while/body/eval_jaxpr/all_to_all | solution.py:55
  33.2 6.4 %fusion.72 = bf16[4,8,2,2048]{3,1,2,0:T(8,128)(2,1)S(1)} fusion(bf16[4,384,2048]{2,1,0:T(8,128)(2,1)} %get-tuple-element.428, bf16[4,2048,384]{2,1,0:T(8,128)(2,1)} %get-tuple-element.427, bf16[8,4,1,2,2048]{4,3,1,0,2:T(2,128)(2,1)S(1)} %bitcast.97, f32[4,8,2,384]{3,1,2,0:T(8,128)S(1)} %fusion.71), kind=kOutput, calls=%fused_computation.6.clone.1 | convolution fusion | flops 201605120 | bytes 13205504 | tf_op jit(solution)/shard_map/while/body/eval_jaxpr/escf,efd->escd/dot_general | solution.py:22
  44.8 6.0 %all-to-all-done.1 = bf16[4,8,2,2048]{3,2,0,1:T(2,128)(2,1)S(1)} async-done(((bf16[4,8,2,2048]{3,2,0,1:T(2,128)(2,1)}), bf16[4,8,2,2048]{3,2,0,1:T(2,128)(2,1)S(1)}, u32[]{:S(2)}, u32[]{:S(2)}) %all-to-all-start.1) | async-done | bytes 262176 | tf_op jit(solution)/shard_map/while/body/eval_jaxpr/all_to_all | solution.py:60
  66.0 5.3 %all-to-all-done = bf16[32,1,2,2048]{3,2,1,0:T(2,128)(2,1)S(1)} async-done(((bf16[32,1,2,2048]{3,2,1,0:T(2,128)(2,1)}), bf16[32,1,2,2048]{3,2,1,0:T(2,128)(2,1)S(1)}, u32[]{:S(2)}, u32[]{:S(2)}) %all-to-all-start) | async-done | bytes 262176 | tf_op jit(solution)/shard_map/while/body/eval_jaxpr/all_to_all | solution.py:55
  75.0 6.4 %fusion.72 = bf16[4,8,2,2048]{3,1,2,0:T(8,128)(2,1)S(1)} fusion(bf16[4,384,2048]{2,1,0:T(8,128)(2,1)} %get-tuple-element.428, bf16[4,2048,384]{2,1,0:T(8,128)(2,1)} %get-tuple-element.427, bf16[8,4,1,2,2048]{4,3,1,0,2:T(2,128)(2,1)S(1)} %bitcast.97, f32[4,8,2,384]{3,1,2,0:T(8,128)S(1)} %fusion.71), kind=kOutput, calls=%fused_computation.6.clone.1 | convolution fusion | flops 201605120 | bytes 13205504 | tf_op jit(solution)/shard_map/while/body/eval_jaxpr/escf,efd->escd/dot_general | solution.py:22
  86.7 6.0 %all-to-all-done.1 = bf16[4,8,2,2048]{3,2,0,1:T(2,128)(2,1)S(1)} async-done(((bf16[4,8,2,2048]{3,2,0,1:T(2,128)(2,1)}), bf16[4,8,2,2048]{3,2,0,1:T(2,128)(2,1)S(1)}, u32[]{:S(2)}, u32[]{:S(2)}) %all-to-all-start.1) | async-done | bytes 262176 | tf_op jit(solution)/shard_map/while/body/eval_jaxpr/all_to_all | solution.py:60
  107.9 5.3 %all-to-all-done = bf16[32,1,2,2048]{3,2,1,0:T(2,128)(2,1)S(1)} async-done(((bf16[32,1,2,2048]{3,2,1,0:T(2,128)(2,1)}), bf16[32,1,2,2048]{3,2,1,0:T(2,128)(2,1)S(1)}, u32[]{:S(2)}, u32[]{:S(2)}) %all-to-all-start) | async-done | bytes 262176 | tf_op jit(solution)/shard_map/while/body/eval_jaxpr/all_to_all | solution.py:55
  116.9 6.4 %fusion.72 = bf16[4,8,2,2048]{3,1,2,0:T(8,128)(2,1)S(1)} fusion(bf16[4,384,2048]{2,1,0:T(8,128)(2,1)} %get-tuple-element.428, bf16[4,2048,384]{2,1,0:T(8,128)(2,1)} %get-tuple-element.427, bf16[8,4,1,2,2048]{4,3,1,0,2:T(2,128)(2,1)S(1)} %bitcast.97, f32[4,8,2,384]{3,1,2,0:T(8,128)S(1)} %fusion.71), kind=kOutput, calls=%fused_computation.6.clone.1 | convolution fusion | flops 201605120 | bytes 13205504 | tf_op jit(solution)/shard_map/while/body/eval_jaxpr/escf,efd->escd/dot_general | solution.py:22
  128.6 6.0 %all-to-all-done.1 = bf16[4,8,2,2048]{3,2,0,1:T(2,128)(2,1)S(1)} async-done(((bf16[4,8,2,2048]{3,2,0,1:T(2,128)(2,1)}), bf16[4,8,2,2048]{3,2,0,1:T(2,128)(2,1)S(1)}, u32[]{:S(2)}, u32[]{:S(2)}) %all-to-all-start.1) | async-done | bytes 262176 | tf_op jit(solution)/shard_map/while/body/eval_jaxpr/all_to_all | solution.py:60
  149.8 5.3 %all-to-all-done = bf16[32,1,2,2048]{3,2,1,0:T(2,128)(2,1)S(1)} async-done(((bf16[32,1,2,2048]{3,2,1,0:T(2,128)(2,1)}), bf16[32,1,2,2048]{3,2,1,0:T(2,128)(2,1)S(1)}, u32[]{:S(2)}, u32[]{:S(2)}) %all-to-all-start) | async-done | bytes 262176 | tf_op jit(solution)/shard_map/while/body/eval_jaxpr/all_to_all | solution.py:55
  158.8 6.4 %fusion.72 = bf16[4,8,2,2048]{3,1,2,0:T(8,128)(2,1)S(1)} fusion(bf16[4,384,2048]{2,1,0:T(8,128)(2,1)} %get-tuple-element.428, bf16[4,2048,384]{2,1,0:T(8,128)(2,1)} %get-tuple-element.427, bf16[8,4,1,2,2048]{4,3,1,0,2:T(2,128)(2,1)S(1)} %bitcast.97, f32[4,8,2,384]{3,1,2,0:T(8,128)S(1)} %fusion.71), kind=kOutput, calls=%fused_computation.6.clone.1 | convolution fusion | flops 201605120 | bytes 13205504 | tf_op jit(solution)/shard_map/while/body/eval_jaxpr/escf,efd->escd/dot_general | solution.py:22
  170.5 6.0 %all-to-all-done.1 = bf16[4,8,2,2048]{3,2,0,1:T(2,128)(2,1)S(1)} async-done(((bf16[4,8,2,2048]{3,2,0,1:T(2,128)(2,1)}), bf16[4,8,2,2048]{3,2,0,1:T(2,128)(2,1)S(1)}, u32[]{:S(2)}, u32[]{:S(2)}) %all-to-all-start.1) | async-done | bytes 262176 | tf_op jit(solution)/shard_map/while/body/eval_jaxpr/all_to_all | solution.py:60
  191.7 5.3 %all-to-all-done = bf16[32,1,2,2048]{3,2,1,0:T(2,128)(2,1)S(1)} async-done(((bf16[32,1,2,2048]{3,2,1,0:T(2,128)(2,1)}), bf16[32,1,2,2048]{3,2,1,0:T(2,128)(2,1)S(1)}, u32[]{:S(2)}, u32[]{:S(2)}) %all-to-all-start) | async-done | bytes 262176 | tf_op jit(solution)/shard_map/while/body/eval_jaxpr/all_to_all | solution.py:55
  200.7 6.4 %fusion.72 = bf16[4,8,2,2048]{3,1,2,0:T(8,128)(2,1)S(1)} fusion(bf16[4,384,2048]{2,1,0:T(8,128)(2,1)} %get-tuple-element.428, bf16[4,2048,384]{2,1,0:T(8,128)(2,1)} %get-tuple-element.427, bf16[8,4,1,2,2048]{4,3,1,0,2:T(2,128)(2,1)S(1)} %bitcast.97, f32[4,8,2,384]{3,1,2,0:T(8,128)S(1)} %fusion.71), kind=kOutput, calls=%fused_computation.6.clone.1 | convolution fusion | flops 201605120 | bytes 13205504 | tf_op jit(solution)/shard_map/while/body/eval_jaxpr/escf,efd->escd/dot_general | solution.py:22
  212.4 6.0 %all-to-all-done.1 = bf16[4,8,2,2048]{3,2,0,1:T(2,128)(2,1)S(1)} async-done(((bf16[4,8,2,2048]{3,2,0,1:T(2,128)(2,1)}), bf16[4,8,2,2048]{3,2,0,1:T(2,128)(2,1)S(1)}, u32[]{:S(2)}, u32[]{:S(2)}) %all-to-all-start.1) | async-done | bytes 262176 | tf_op jit(solution)/shard_map/while/body/eval_jaxpr/all_to_all | solution.py:60
  233.5 5.3 %all-to-all-done = bf16[32,1,2,2048]{3,2,1,0:T(2,128)(2,1)S(1)} async-done(((bf16[32,1,2,2048]{3,2,1,0:T(2,128)(2,1)}), bf16[32,1,2,2048]{3,2,1,0:T(2,128)(2,1)S(1)}, u32[]{:S(2)}, u32[]{:S(2)}) %all-to-all-start) | async-done | bytes 262176 | tf_op jit(solution)/shard_map/while/body/eval_jaxpr/all_to_all | solution.py:55
  242.6 6.4 %fusion.72 = bf16[4,8,2,2048]{3,1,2,0:T(8,128)(2,1)S(1)} fusion(bf16[4,384,2048]{2,1,0:T(8,128)(2,1)} %get-tuple-element.428, bf16[4,2048,384]{2,1,0:T(8,128)(2,1)} %get-tuple-element.427, bf16[8,4,1,2,2048]{4,3,1,0,2:T(2,128)(2,1)S(1)} %bitcast.97, f32[4,8,2,384]{3,1,2,0:T(8,128)S(1)} %fusion.71), kind=kOutput, calls=%fused_computation.6.clone.1 | convolution fusion | flops 201605120 | bytes 13205504 | tf_op jit(solution)/shard_map/while/body/eval_jaxpr/escf,efd->escd/dot_general | solution.py:22
  254.2 6.0 %all-to-all-done.1 = bf16[4,8,2,2048]{3,2,0,1:T(2,128)(2,1)S(1)} async-done(((bf16[4,8,2,2048]{3,2,0,1:T(2,128)(2,1)}), bf16[4,8,2,2048]{3,2,0,1:T(2,128)(2,1)S(1)}, u32[]{:S(2)}, u32[]{:S(2)}) %all-to-all-start.1) | async-done | bytes 262176 | tf_op jit(solution)/shard_map/while/body/eval_jaxpr/all_to_all | solution.py:60
  275.4 5.3 %all-to-all-done = bf16[32,1,2,2048]{3,2,1,0:T(2,128)(2,1)S(1)} async-done(((bf16[32,1,2,2048]{3,2,1,0:T(2,128)(2,1)}), bf16[32,1,2,2048]{3,2,1,0:T(2,128)(2,1)S(1)}, u32[]{:S(2)}, u32[]{:S(2)}) %all-to-all-start) | async-done | bytes 262176 | tf_op jit(solution)/shard_map/while/body/eval_jaxpr/all_to_all | solution.py:55
  284.4 6.4 %fusion.72 = bf16[4,8,2,2048]{3,1,2,0:T(8,128)(2,1)S(1)} fusion(bf16[4,384,2048]{2,1,0:T(8,128)(2,1)} %get-tuple-element.428, bf16[4,2048,384]{2,1,0:T(8,128)(2,1)} %get-tuple-element.427, bf16[8,4,1,2,2048]{4,3,1,0,2:T(2,128)(2,1)S(1)} %bitcast.97, f32[4,8,2,384]{3,1,2,0:T(8,128)S(1)} %fusion.71), kind=kOutput, calls=%fused_computation.6.clone.1 | convolution fusion | flops 201605120 | bytes 13205504 | tf_op jit(solution)/shard_map/while/body/eval_jaxpr/escf,efd->escd/dot_general | solution.py:22
  296.1 6.0 %all-to-all-done.1 = bf16[4,8,2,2048]{3,2,0,1:T(2,128)(2,1)S(1)} async-done(((bf16[4,8,2,2048]{3,2,0,1:T(2,128)(2,1)}), bf16[4,8,2,2048]{3,2,0,1:T(2,128)(2,1)S(1)}, u32[]{:S(2)}, u32[]{:S(2)}) %all-to-all-start.1) | async-done | bytes 262176 | tf_op jit(solution)/shard_map/while/body/eval_jaxpr/all_to_all | solution.py:60
  326.3 6.4 %fusion.72 = bf16[4,8,2,2048]{3,1,2,0:T(8,128)(2,1)S(1)} fusion(bf16[4,384,2048]{2,1,0:T(8,128)(2,1)} %get-tuple-element.428, bf16[4,2048,384]{2,1,0:T(8,128)(2,1)} %get-tuple-element.427, bf16[8,4,1,2,2048]{4,3,1,0,2:T(2,128)(2,1)S(1)} %bitcast.97, f32[4,8,2,384]{3,1,2,0:T(8,128)S(1)} %fusion.71), kind=kOutput, calls=%fused_computation.6.clone.1 | convolution fusion | flops 201605120 | bytes 13205504 | tf_op jit(solution)/shard_map/while/body/eval_jaxpr/escf,efd->escd/dot_general | solution.py:22
  338.0 6.0 %all-to-all-done.1 = bf16[4,8,2,2048]{3,2,0,1:T(2,128)(2,1)S(1)} async-done(((bf16[4,8,2,2048]{3,2,0,1:T(2,128)(2,1)}), bf16[4,8,2,2048]{3,2,0,1:T(2,128)(2,1)S(1)}, u32[]{:S(2)}, u32[]{:S(2)}) %all-to-all-start.1) | async-done | bytes 262176 | tf_op jit(solution)/shard_map/while/body/eval_jaxpr/all_to_all | solution.py:60
  359.2 5.3 %all-to-all-done = bf16[32,1,2,2048]{3,2,1,0:T(2,128)(2,1)S(1)} async-done(((bf16[32,1,2,2048]{3,2,1,0:T(2,128)(2,1)}), bf16[32,1,2,2048]{3,2,1,0:T(2,128)(2,1)S(1)}, u32[]{:S(2)}, u32[]{:S(2)}) %all-to-all-start) | async-done | bytes 262176 | tf_op jit(solution)/shard_map/while/body/eval_jaxpr/all_to_all | solution.py:55
  368.2 6.4 %fusion.72 = bf16[4,8,2,2048]{3,1,2,0:T(8,128)(2,1)S(1)} fusion(bf16[4,384,2048]{2,1,0:T(8,128)(2,1)} %get-tuple-element.428, bf16[4,2048,384]{2,1,0:T(8,128)(2,1)} %get-tuple-element.427, bf16[8,4,1,2,2048]{4,3,1,0,2:T(2,128)(2,1)S(1)} %bitcast.97, f32[4,8,2,384]{3,1,2,0:T(8,128)S(1)} %fusion.71), kind=kOutput, calls=%fused_computation.6.clone.1 | convolution fusion | flops 201605120 | bytes 13205504 | tf_op jit(solution)/shard_map/while/body/eval_jaxpr/escf,efd->escd/dot_general | solution.py:22
  379.9 6.0 %all-to-all-done.1 = bf16[4,8,2,2048]{3,2,0,1:T(2,128)(2,1)S(1)} async-done(((bf16[4,8,2,2048]{3,2,0,1:T(2,128)(2,1)}), bf16[4,8,2,2048]{3,2,0,1:T(2,128)(2,1)S(1)}, u32[]{:S(2)}, u32[]{:S(2)}) %all-to-all-start.1) | async-done | bytes 262176 | tf_op jit(solution)/shard_map/while/body/eval_jaxpr/all_to_all | solution.py:60
  410.1 6.4 %fusion.72 = bf16[4,8,2,2048]{3,1,2,0:T(8,128)(2,1)S(1)} fusion(bf16[4,384,2048]{2,1,0:T(8,128)(2,1)} %get-tuple-element.428, bf16[4,2048,384]{2,1,0:T(8,128)(2,1)} %get-tuple-element.427, bf16[8,4,1,2,2048]{4,3,1,0,2:T(2,128)(2,1)S(1)} %bitcast.97, f32[4,8,2,384]{3,1,2,0:T(8,128)S(1)} %fusion.71), kind=kOutput, calls=%fused_computation.6.clone.1 | convolution fusion | flops 201605120 | bytes 13205504 | tf_op jit(solution)/shard_map/while/body/eval_jaxpr/escf,efd->escd/dot_general | solution.py:22
  421.7 6.0 %all-to-all-done.1 = bf16[4,8,2,2048]{3,2,0,1:T(2,128)(2,1)S(1)} async-done(((bf16[4,8,2,2048]{3,2,0,1:T(2,128)(2,1)}), bf16[4,8,2,2048]{3,2,0,1:T(2,128)(2,1)S(1)}, u32[]{:S(2)}, u32[]{:S(2)}) %all-to-all-start.1) | async-done | bytes 262176 | tf_op jit(solution)/shard_map/while/body/eval_jaxpr/all_to_all | solution.py:60
  451.9 6.4 %fusion.72 = bf16[4,8,2,2048]{3,1,2,0:T(8,128)(2,1)S(1)} fusion(bf16[4,384,2048]{2,1,0:T(8,128)(2,1)} %get-tuple-element.428, bf16[4,2048,384]{2,1,0:T(8,128)(2,1)} %get-tuple-element.427, bf16[8,4,1,2,2048]{4,3,1,0,2:T(2,128)(2,1)S(1)} %bitcast.97, f32[4,8,2,384]{3,1,2,0:T(8,128)S(1)} %fusion.71), kind=kOutput, calls=%fused_computation.6.clone.1 | convolution fusion | flops 201605120 | bytes 13205504 | tf_op jit(solution)/shard_map/while/body/eval_jaxpr/escf,efd->escd/dot_general | solution.py:22
  463.6 6.0 %all-to-all-done.1 = bf16[4,8,2,2048]{3,2,0,1:T(2,128)(2,1)S(1)} async-done(((bf16[4,8,2,2048]{3,2,0,1:T(2,128)(2,1)}), bf16[4,8,2,2048]{3,2,0,1:T(2,128)(2,1)S(1)}, u32[]{:S(2)}, u32[]{:S(2)}) %all-to-all-start.1) | async-done | bytes 262176 | tf_op jit(solution)/shard_map/while/body/eval_jaxpr/all_to_all | solution.py:60
  (282 shorter events, 282.2 us)
Async XLA Ops:
  18.8 10.7 %all-to-all-start = ((bf16[32,1,2,2048]{3,2,1,0:T(2,128)(2,1)}), bf16[32,1,2,2048]{3,2,1,0:T(2,128)(2,1)S(1)}, u32[]{:S(2)}, u32[]{:S(2)}) async-start(bf16[32,1,2,2048]{3,2,1,0:T(2,128)(2,1)} %bitcast.90), calls=%async_computation | async-start | bytes 524288 | tf_op jit(solution)/shard_map/while/body/eval_jaxpr/all_to_all | solution.py:55
  40.6 10.3 %all-to-all-start.1 = ((bf16[4,8,2,2048]{3,2,0,1:T(2,128)(2,1)}), bf16[4,8,2,2048]{3,2,0,1:T(2,128)(2,1)S(1)}, u32[]{:S(2)}, u32[]{:S(2)}) async-start(bf16[4,8,2,2048]{3,2,0,1:T(2,128)(2,1)} %copy.33), calls=%async_computation.1 | async-start | bytes 524288 | tf_op jit(solution)/shard_map/while/body/eval_jaxpr/all_to_all | solution.py:60
  51.2 5.8 %collective-permute-start = (bf16[8,2048]{1,0:T(8,128)(2,1)S(1)}, bf16[8,2048]{1,0:T(8,128)(2,1)S(1)}, u32[]{:S(2)}, u32[]{:S(2)}) collective-permute-start(bf16[8,2048]{1,0:T(8,128)(2,1)S(1)} %get-tuple-element.383), channel_id=1, source_target_pairs={{0,8},{8,16},{16,24},{1,9},{9,17},{17,25},{2,10},{10,18},{18,26},{... | collective-permute-start | bytes 98312 | tf_op jit(solution)/shard_map/while/body/eval_jaxpr/ppermute | solution.py:15
  61.0 10.3 %all-to-all-start = ((bf16[32,1,2,2048]{3,2,1,0:T(2,128)(2,1)}), bf16[32,1,2,2048]{3,2,1,0:T(2,128)(2,1)S(1)}, u32[]{:S(2)}, u32[]{:S(2)}) async-start(bf16[32,1,2,2048]{3,2,1,0:T(2,128)(2,1)} %bitcast.90), calls=%async_computation | async-start | bytes 524288 | tf_op jit(solution)/shard_map/while/body/eval_jaxpr/all_to_all | solution.py:55
  82.4 10.3 %all-to-all-start.1 = ((bf16[4,8,2,2048]{3,2,0,1:T(2,128)(2,1)}), bf16[4,8,2,2048]{3,2,0,1:T(2,128)(2,1)S(1)}, u32[]{:S(2)}, u32[]{:S(2)}) async-start(bf16[4,8,2,2048]{3,2,0,1:T(2,128)(2,1)} %copy.33), calls=%async_computation.1 | async-start | bytes 524288 | tf_op jit(solution)/shard_map/while/body/eval_jaxpr/all_to_all | solution.py:60
  93.1 5.8 %collective-permute-start = (bf16[8,2048]{1,0:T(8,128)(2,1)S(1)}, bf16[8,2048]{1,0:T(8,128)(2,1)S(1)}, u32[]{:S(2)}, u32[]{:S(2)}) collective-permute-start(bf16[8,2048]{1,0:T(8,128)(2,1)S(1)} %get-tuple-element.383), channel_id=1, source_target_pairs={{0,8},{8,16},{16,24},{1,9},{9,17},{17,25},{2,10},{10,18},{18,26},{... | collective-permute-start | bytes 98312 | tf_op jit(solution)/shard_map/while/body/eval_jaxpr/ppermute | solution.py:15
  102.9 10.3 %all-to-all-start = ((bf16[32,1,2,2048]{3,2,1,0:T(2,128)(2,1)}), bf16[32,1,2,2048]{3,2,1,0:T(2,128)(2,1)S(1)}, u32[]{:S(2)}, u32[]{:S(2)}) async-start(bf16[32,1,2,2048]{3,2,1,0:T(2,128)(2,1)} %bitcast.90), calls=%async_computation | async-start | bytes 524288 | tf_op jit(solution)/shard_map/while/body/eval_jaxpr/all_to_all | solution.py:55
  124.3 10.3 %all-to-all-start.1 = ((bf16[4,8,2,2048]{3,2,0,1:T(2,128)(2,1)}), bf16[4,8,2,2048]{3,2,0,1:T(2,128)(2,1)S(1)}, u32[]{:S(2)}, u32[]{:S(2)}) async-start(bf16[4,8,2,2048]{3,2,0,1:T(2,128)(2,1)} %copy.33), calls=%async_computation.1 | async-start | bytes 524288 | tf_op jit(solution)/shard_map/while/body/eval_jaxpr/all_to_all | solution.py:60
  134.9 5.8 %collective-permute-start = (bf16[8,2048]{1,0:T(8,128)(2,1)S(1)}, bf16[8,2048]{1,0:T(8,128)(2,1)S(1)}, u32[]{:S(2)}, u32[]{:S(2)}) collective-permute-start(bf16[8,2048]{1,0:T(8,128)(2,1)S(1)} %get-tuple-element.383), channel_id=1, source_target_pairs={{0,8},{8,16},{16,24},{1,9},{9,17},{17,25},{2,10},{10,18},{18,26},{... | collective-permute-start | bytes 98312 | tf_op jit(solution)/shard_map/while/body/eval_jaxpr/ppermute | solution.py:15
  144.8 10.3 %all-to-all-start = ((bf16[32,1,2,2048]{3,2,1,0:T(2,128)(2,1)}), bf16[32,1,2,2048]{3,2,1,0:T(2,128)(2,1)S(1)}, u32[]{:S(2)}, u32[]{:S(2)}) async-start(bf16[32,1,2,2048]{3,2,1,0:T(2,128)(2,1)} %bitcast.90), calls=%async_computation | async-start | bytes 524288 | tf_op jit(solution)/shard_map/while/body/eval_jaxpr/all_to_all | solution.py:55
  166.2 10.3 %all-to-all-start.1 = ((bf16[4,8,2,2048]{3,2,0,1:T(2,128)(2,1)}), bf16[4,8,2,2048]{3,2,0,1:T(2,128)(2,1)S(1)}, u32[]{:S(2)}, u32[]{:S(2)}) async-start(bf16[4,8,2,2048]{3,2,0,1:T(2,128)(2,1)} %copy.33), calls=%async_computation.1 | async-start | bytes 524288 | tf_op jit(solution)/shard_map/while/body/eval_jaxpr/all_to_all | solution.py:60
  176.8 5.8 %collective-permute-start = (bf16[8,2048]{1,0:T(8,128)(2,1)S(1)}, bf16[8,2048]{1,0:T(8,128)(2,1)S(1)}, u32[]{:S(2)}, u32[]{:S(2)}) collective-permute-start(bf16[8,2048]{1,0:T(8,128)(2,1)S(1)} %get-tuple-element.383), channel_id=1, source_target_pairs={{0,8},{8,16},{16,24},{1,9},{9,17},{17,25},{2,10},{10,18},{18,26},{... | collective-permute-start | bytes 98312 | tf_op jit(solution)/shard_map/while/body/eval_jaxpr/ppermute | solution.py:15
  186.7 10.3 %all-to-all-start = ((bf16[32,1,2,2048]{3,2,1,0:T(2,128)(2,1)}), bf16[32,1,2,2048]{3,2,1,0:T(2,128)(2,1)S(1)}, u32[]{:S(2)}, u32[]{:S(2)}) async-start(bf16[32,1,2,2048]{3,2,1,0:T(2,128)(2,1)} %bitcast.90), calls=%async_computation | async-start | bytes 524288 | tf_op jit(solution)/shard_map/while/body/eval_jaxpr/all_to_all | solution.py:55
  208.1 10.3 %all-to-all-start.1 = ((bf16[4,8,2,2048]{3,2,0,1:T(2,128)(2,1)}), bf16[4,8,2,2048]{3,2,0,1:T(2,128)(2,1)S(1)}, u32[]{:S(2)}, u32[]{:S(2)}) async-start(bf16[4,8,2,2048]{3,2,0,1:T(2,128)(2,1)} %copy.33), calls=%async_computation.1 | async-start | bytes 524288 | tf_op jit(solution)/shard_map/while/body/eval_jaxpr/all_to_all | solution.py:60
  218.7 5.8 %collective-permute-start = (bf16[8,2048]{1,0:T(8,128)(2,1)S(1)}, bf16[8,2048]{1,0:T(8,128)(2,1)S(1)}, u32[]{:S(2)}, u32[]{:S(2)}) collective-permute-start(bf16[8,2048]{1,0:T(8,128)(2,1)S(1)} %get-tuple-element.383), channel_id=1, source_target_pairs={{0,8},{8,16},{16,24},{1,9},{9,17},{17,25},{2,10},{10,18},{18,26},{... | collective-permute-start | bytes 98312 | tf_op jit(solution)/shard_map/while/body/eval_jaxpr/ppermute | solution.py:15
  228.5 10.3 %all-to-all-start = ((bf16[32,1,2,2048]{3,2,1,0:T(2,128)(2,1)}), bf16[32,1,2,2048]{3,2,1,0:T(2,128)(2,1)S(1)}, u32[]{:S(2)}, u32[]{:S(2)}) async-start(bf16[32,1,2,2048]{3,2,1,0:T(2,128)(2,1)} %bitcast.90), calls=%async_computation | async-start | bytes 524288 | tf_op jit(solution)/shard_map/while/body/eval_jaxpr/all_to_all | solution.py:55
  249.9 10.3 %all-to-all-start.1 = ((bf16[4,8,2,2048]{3,2,0,1:T(2,128)(2,1)}), bf16[4,8,2,2048]{3,2,0,1:T(2,128)(2,1)S(1)}, u32[]{:S(2)}, u32[]{:S(2)}) async-start(bf16[4,8,2,2048]{3,2,0,1:T(2,128)(2,1)} %copy.33), calls=%async_computation.1 | async-start | bytes 524288 | tf_op jit(solution)/shard_map/while/body/eval_jaxpr/all_to_all | solution.py:60
  260.6 5.8 %collective-permute-start = (bf16[8,2048]{1,0:T(8,128)(2,1)S(1)}, bf16[8,2048]{1,0:T(8,128)(2,1)S(1)}, u32[]{:S(2)}, u32[]{:S(2)}) collective-permute-start(bf16[8,2048]{1,0:T(8,128)(2,1)S(1)} %get-tuple-element.383), channel_id=1, source_target_pairs={{0,8},{8,16},{16,24},{1,9},{9,17},{17,25},{2,10},{10,18},{18,26},{... | collective-permute-start | bytes 98312 | tf_op jit(solution)/shard_map/while/body/eval_jaxpr/ppermute | solution.py:15
  270.4 10.3 %all-to-all-start = ((bf16[32,1,2,2048]{3,2,1,0:T(2,128)(2,1)}), bf16[32,1,2,2048]{3,2,1,0:T(2,128)(2,1)S(1)}, u32[]{:S(2)}, u32[]{:S(2)}) async-start(bf16[32,1,2,2048]{3,2,1,0:T(2,128)(2,1)} %bitcast.90), calls=%async_computation | async-start | bytes 524288 | tf_op jit(solution)/shard_map/while/body/eval_jaxpr/all_to_all | solution.py:55
  291.8 10.3 %all-to-all-start.1 = ((bf16[4,8,2,2048]{3,2,0,1:T(2,128)(2,1)}), bf16[4,8,2,2048]{3,2,0,1:T(2,128)(2,1)S(1)}, u32[]{:S(2)}, u32[]{:S(2)}) async-start(bf16[4,8,2,2048]{3,2,0,1:T(2,128)(2,1)} %copy.33), calls=%async_computation.1 | async-start | bytes 524288 | tf_op jit(solution)/shard_map/while/body/eval_jaxpr/all_to_all | solution.py:60
  302.4 5.8 %collective-permute-start = (bf16[8,2048]{1,0:T(8,128)(2,1)S(1)}, bf16[8,2048]{1,0:T(8,128)(2,1)S(1)}, u32[]{:S(2)}, u32[]{:S(2)}) collective-permute-start(bf16[8,2048]{1,0:T(8,128)(2,1)S(1)} %get-tuple-element.383), channel_id=1, source_target_pairs={{0,8},{8,16},{16,24},{1,9},{9,17},{17,25},{2,10},{10,18},{18,26},{... | collective-permute-start | bytes 98312 | tf_op jit(solution)/shard_map/while/body/eval_jaxpr/ppermute | solution.py:15
  312.3 10.3 %all-to-all-start = ((bf16[32,1,2,2048]{3,2,1,0:T(2,128)(2,1)}), bf16[32,1,2,2048]{3,2,1,0:T(2,128)(2,1)S(1)}, u32[]{:S(2)}, u32[]{:S(2)}) async-start(bf16[32,1,2,2048]{3,2,1,0:T(2,128)(2,1)} %bitcast.90), calls=%async_computation | async-start | bytes 524288 | tf_op jit(solution)/shard_map/while/body/eval_jaxpr/all_to_all | solution.py:55
  333.7 10.3 %all-to-all-start.1 = ((bf16[4,8,2,2048]{3,2,0,1:T(2,128)(2,1)}), bf16[4,8,2,2048]{3,2,0,1:T(2,128)(2,1)S(1)}, u32[]{:S(2)}, u32[]{:S(2)}) async-start(bf16[4,8,2,2048]{3,2,0,1:T(2,128)(2,1)} %copy.33), calls=%async_computation.1 | async-start | bytes 524288 | tf_op jit(solution)/shard_map/while/body/eval_jaxpr/all_to_all | solution.py:60
  344.3 5.8 %collective-permute-start = (bf16[8,2048]{1,0:T(8,128)(2,1)S(1)}, bf16[8,2048]{1,0:T(8,128)(2,1)S(1)}, u32[]{:S(2)}, u32[]{:S(2)}) collective-permute-start(bf16[8,2048]{1,0:T(8,128)(2,1)S(1)} %get-tuple-element.383), channel_id=1, source_target_pairs={{0,8},{8,16},{16,24},{1,9},{9,17},{17,25},{2,10},{10,18},{18,26},{... | collective-permute-start | bytes 98312 | tf_op jit(solution)/shard_map/while/body/eval_jaxpr/ppermute | solution.py:15
  354.2 10.3 %all-to-all-start = ((bf16[32,1,2,2048]{3,2,1,0:T(2,128)(2,1)}), bf16[32,1,2,2048]{3,2,1,0:T(2,128)(2,1)S(1)}, u32[]{:S(2)}, u32[]{:S(2)}) async-start(bf16[32,1,2,2048]{3,2,1,0:T(2,128)(2,1)} %bitcast.90), calls=%async_computation | async-start | bytes 524288 | tf_op jit(solution)/shard_map/while/body/eval_jaxpr/all_to_all | solution.py:55
  375.6 10.3 %all-to-all-start.1 = ((bf16[4,8,2,2048]{3,2,0,1:T(2,128)(2,1)}), bf16[4,8,2,2048]{3,2,0,1:T(2,128)(2,1)S(1)}, u32[]{:S(2)}, u32[]{:S(2)}) async-start(bf16[4,8,2,2048]{3,2,0,1:T(2,128)(2,1)} %copy.33), calls=%async_computation.1 | async-start | bytes 524288 | tf_op jit(solution)/shard_map/while/body/eval_jaxpr/all_to_all | solution.py:60
  386.2 5.8 %collective-permute-start = (bf16[8,2048]{1,0:T(8,128)(2,1)S(1)}, bf16[8,2048]{1,0:T(8,128)(2,1)S(1)}, u32[]{:S(2)}, u32[]{:S(2)}) collective-permute-start(bf16[8,2048]{1,0:T(8,128)(2,1)S(1)} %get-tuple-element.383), channel_id=1, source_target_pairs={{0,8},{8,16},{16,24},{1,9},{9,17},{17,25},{2,10},{10,18},{18,26},{... | collective-permute-start | bytes 98312 | tf_op jit(solution)/shard_map/while/body/eval_jaxpr/ppermute | solution.py:15
  396.0 10.3 %all-to-all-start = ((bf16[32,1,2,2048]{3,2,1,0:T(2,128)(2,1)}), bf16[32,1,2,2048]{3,2,1,0:T(2,128)(2,1)S(1)}, u32[]{:S(2)}, u32[]{:S(2)}) async-start(bf16[32,1,2,2048]{3,2,1,0:T(2,128)(2,1)} %bitcast.90), calls=%async_computation | async-start | bytes 524288 | tf_op jit(solution)/shard_map/while/body/eval_jaxpr/all_to_all | solution.py:55
  417.5 10.3 %all-to-all-start.1 = ((bf16[4,8,2,2048]{3,2,0,1:T(2,128)(2,1)}), bf16[4,8,2,2048]{3,2,0,1:T(2,128)(2,1)S(1)}, u32[]{:S(2)}, u32[]{:S(2)}) async-start(bf16[4,8,2,2048]{3,2,0,1:T(2,128)(2,1)} %copy.33), calls=%async_computation.1 | async-start | bytes 524288 | tf_op jit(solution)/shard_map/while/body/eval_jaxpr/all_to_all | solution.py:60
  437.9 10.3 %all-to-all-start = ((bf16[32,1,2,2048]{3,2,1,0:T(2,128)(2,1)}), bf16[32,1,2,2048]{3,2,1,0:T(2,128)(2,1)S(1)}, u32[]{:S(2)}, u32[]{:S(2)}) async-start(bf16[32,1,2,2048]{3,2,1,0:T(2,128)(2,1)} %bitcast.90), calls=%async_computation | async-start | bytes 524288 | tf_op jit(solution)/shard_map/while/body/eval_jaxpr/all_to_all | solution.py:55
  459.3 10.3 %all-to-all-start.1 = ((bf16[4,8,2,2048]{3,2,0,1:T(2,128)(2,1)}), bf16[4,8,2,2048]{3,2,0,1:T(2,128)(2,1)S(1)}, u32[]{:S(2)}, u32[]{:S(2)}) async-start(bf16[4,8,2,2048]{3,2,0,1:T(2,128)(2,1)} %copy.33), calls=%async_computation.1 | async-start | bytes 524288 | tf_op jit(solution)/shard_map/while/body/eval_jaxpr/all_to_all | solution.py:60
  470.0 5.8 %collective-permute-start = (bf16[8,2048]{1,0:T(8,128)(2,1)S(1)}, bf16[8,2048]{1,0:T(8,128)(2,1)S(1)}, u32[]{:S(2)}, u32[]{:S(2)}) collective-permute-start(bf16[8,2048]{1,0:T(8,128)(2,1)S(1)} %get-tuple-element.383), channel_id=1, source_target_pairs={{0,8},{8,16},{16,24},{1,9},{9,17},{17,25},{2,10},{10,18},{18,26},{... | collective-permute-start | bytes 98312 | tf_op jit(solution)/shard_map/while/body/eval_jaxpr/ppermute | solution.py:15
  (2 other events, 6.5 us)
where the time goes:
time: 483 us; the launch traced here: 476 us
  waiting for transfers between devices  174 us (36%)
  matrix products  125 us (26%)
  starting transfers between devices  89.6 us (19%)
  other arithmetic  40.3 us (8%)
  local copies, waits for them, and re-layouts  32.6 us (7%)
  blocking collectives  14.7 us (3%)
    dot_general x11, matrix products, expert_block(): jnp.einsum('escf,efd->escd', active, w_down, preferred_element_type=jnp.f...  70.4 us
    all_to_all x11, waiting for transfers between devices, moe_layer(): lax.all_to_all(results, 'expert', split_axis=1, concat_axis=0, tiled=True)  66 us
    all_to_all x11, waiting for transfers between devices, moe_layer(): lax.all_to_all(sending, 'expert', split_axis=0, concat_axis=1, tiled=True)  58.2 us
    ppermute x11, waiting for transfers between devices, passed_along(): return lax.ppermute(value, axis, pairs)  49.6 us
    dot_general x11, matrix products, expert_block(): jnp.einsum('escd,edf->escf', routed, w_gate, preferred_element_type=jnp.f...  41.1 us
    all_to_all x11, starting transfers between devices, moe_layer(): lax.all_to_all(sending, 'expert', split_axis=0, concat_axis=1, tiled=True)  37.8 us
    all_to_all x11, starting transfers between devices, moe_layer(): lax.all_to_all(results, 'expert', split_axis=1, concat_axis=0, tiled=True)  37.5 us
    all_gather x1, blocking collectives, local(): full_tokens = lax.all_gather(tokens, 'section', axis=2, tiled=True)  14.7 us
  transfers between devices with their start and end apart: 33, of which 33 were waited for; matrix products, arithmetic and copies ran while one was open for 6% of the time, Pallas kernels for 0%

commit v1 on v0

v1 whole, which is shorter than its diff:
```python
import functools

import jax
import jax.numpy as jnp
from jax import lax
from jax.experimental import pallas as pl
from jax.experimental.pallas import tpu as pltpu
from jax.sharding import PartitionSpec as P

EPS = 1e-06
GROUP = 2
MESH = pl.DeviceIdType.MESH
LANES = 128


def kernel(
    sections, peers, experts_local,
    tokens, gain, gate_hbm, up_hbm, down_hbm, ids, probs,
    out,
    w_gate, w_up, w_down, x_in, normed, active, partial, pair_in, pair_out, returned, shares,
    weight_sem, token_send, token_recv, share_send, share_recv, gather_send, gather_recv,
    forward_send, pair_send, pair_recv, return_send, return_recv, pass_send, pass_recv,
):
    groups, rows, width = x_in.shape
    chips = peers // 2
    ff = gate_hbm.shape[2]
    hidden = experts_local * ff
    experts = experts_local * peers
    part = tokens.shape[2]
    section = lax.axis_index("section")
    index = lax.axis_index("expert")
    chip, core = lax.div(index, 2), lax.rem(index, 2)
    other = 1 - core
    sibling = chip * 2 + other

    def slot_of(chip_index, core_index):
        return core_index * chips + chip_index

    mine = slot_of(chip, core)

    def weight_copies(which):
        copies = []
        for e in range(experts_local):
            span = pl.ds(e * ff, ff)
            if which < 2:
                source, target = ((gate_hbm, w_gate), (up_hbm, w_up))[which]
                copies.append(pltpu.make_async_copy(
                    source.at[e], target.at[:, span], weight_sem.at[which, e]))
            else:
                copies.append(pltpu.make_async_copy(
                    down_hbm.at[e], w_down.at[span], weight_sem.at[which, e]))
        return copies

    for copy in weight_copies(0) + weight_copies(1) + weight_copies(2):
        copy.start()

    def remote(source, target, send, recv, device):
        return pltpu.make_async_remote_copy(
            src_ref=source, dst_ref=target, send_sem=send, recv_sem=recv,
            device_id=device, device_id_type=MESH)

    def at_peer(peer):
        return {"section": section, "expert": peer}

    def at_section(which):
        return {"section": which, "expert": index}

    barrier = pltpu.get_barrier_semaphore()
    for step in range(1, peers):
        pl.semaphore_signal(barrier, inc=1, device_id=at_peer(lax.rem(index + step, peers)),
                            device_id_type=MESH)
    for step in range(1, sections):
        pl.semaphore_signal(barrier, inc=1,
                            device_id=at_section(lax.rem(section + step, sections)),
                            device_id_type=MESH)
    pl.semaphore_wait(barrier, peers + sections - 2)

    def token_copy(g, origin):
        columns = pl.ds(pl.multiple_of(origin * part, part), part)
        return remote(tokens.at[g], x_in.at[g, :, columns], token_send.at[g],
                      token_recv.at[g, origin], at_section(0))

    @pl.when(section > 0)
    def _():
        for g in range(groups):
            token_copy(g, section).start()

    lane = lax.broadcasted_iota(jnp.int32, (rows, LANES), 1)
    spread = jnp.zeros((rows, LANES), jnp.float32)
    top = ids.shape[2]
    for g in range(groups):
        share = probs[g] / jnp.sum(probs[g], axis=-1, keepdims=True)
        named = ids[g] + g * experts
        for k in range(top):
            spread += jnp.where(named[:, k:k + 1] == lane, share[:, k:k + 1], 0.0)
    shares[mine] = spread

    def share_copy(step):
        target = lax.rem(index + step, peers)
        return remote(shares.at[mine], shares.at[mine], share_send.at[step],
                      share_recv.at[mine], at_peer(target))

    def gather_copy(g, step):
        target = lax.rem(chip + step, chips) * 2 + core
        return remote(normed.at[g, mine], normed.at[g, mine], gather_send.at[g, step],
                      gather_recv.at[g, mine], at_peer(target))

    def sibling_copy(g):
        return remote(normed.at[g, mine], normed.at[g, mine], gather_send.at[g, 0],
                      gather_recv.at[g, mine], at_peer(sibling))

    def forward_copy(g, step):
        slot = slot_of(lax.rem(chip + step, chips), core)
        return remote(normed.at[g, slot], normed.at[g, slot], forward_send.at[g, step],
                      gather_recv.at[g, slot], at_peer(sibling))

    def gather_arrival(g, slot):
        return remote(normed.at[g, slot], normed.at[g, slot], gather_send.at[g, 0],
                      gather_recv.at[g, slot], at_peer(sibling))

    def pair_copy(g):
        return remote(partial.at[g, pl.ds(other * chips, chips)], pair_in.at[g],
                      pair_send.at[g], pair_recv.at[g], at_peer(sibling))

    def return_copy(g, step):
        target = lax.rem(chip + step, chips)
        return remote(pair_out.at[g, target], returned.at[g, chip], return_send.at[g, step],
                      return_recv.at[g, chip], at_peer(target * 2 + core))

    def return_arrival(g, origin):
        return remote(pair_out.at[g, origin], returned.at[g, origin], return_send.at[g, 0],
                      return_recv.at[g, origin], at_peer(sibling))

    def pass_copy(g):
        return remote(out.at[g], x_in.at[g], pass_send.at[g], pass_recv.at[g],
                      at_section(lax.rem(section + 1, sections)))

    def enter(g):
        @pl.when(section == 0)
        def _():
            x_in[g, :, pl.ds(0, part)] = tokens[g]
            for origin in range(1, sections):
                token_copy(g, origin).wait_recv()

        @pl.when(section > 0)
        def _():
            pass_copy(g).wait_recv()

        wide = x_in[g].astype(jnp.float32)
        scale = lax.rsqrt(jnp.mean(wide * wide, axis=-1, keepdims=True) + EPS)
        normed[g, mine] = (wide * scale * gain[...]).astype(jnp.bfloat16)
        for step in range(1, chips):
            gather_copy(g, step).start()
        sibling_copy(g).start()

    def forward(g):
        for step in range(1, chips):
            gather_arrival(g, slot_of(lax.rem(chip + step, chips), core)).wait_recv()
            forward_copy(g, step).start()

    total_rows = peers * rows
    tile = 256 if hidden % 256 == 0 else LANES
    wide_lane = lax.broadcasted_iota(jnp.int32, (total_rows, LANES), 1)

    def experts_block(g):
        for step in range(chips):
            gather_arrival(g, slot_of(lax.rem(chip + step, chips), other)).wait_recv()

        @pl.when(g == 0)
        def _():
            for copy in weight_copies(0) + weight_copies(1):
                copy.wait()
            for step in range(1, peers):
                origin = lax.rem(index + step, peers)
                slot = slot_of(lax.div(origin, 2), lax.rem(origin, 2))
                remote(shares.at[slot], shares.at[slot], share_send.at[step],
                       share_recv.at[slot], at_peer(origin)).wait_recv()

        every = shares[...].reshape(total_rows, LANES)
        factor = []
        for e in range(experts_local):
            pick = wide_lane == g * experts + index * experts_local + e
            factor.append(jnp.sum(jnp.where(pick, every, 0.0), axis=-1, keepdims=True))
        rows_in = normed[g].reshape(total_rows, width)
        for start in range(0, hidden, tile):
            columns = pl.ds(start, tile)
            gate = jnp.dot(rows_in, w_gate[:, columns], preferred_element_type=jnp.float32)
            up = jnp.dot(rows_in, w_up[:, columns], preferred_element_type=jnp.float32)
            mid = gate / (1.0 + jnp.exp(-gate)) * up
            for begin in range(0, tile, LANES):
                piece = mid[:, begin:begin + LANES] * factor[(start + begin) // ff]
                active[:, pl.ds(start + begin, LANES)] = piece.astype(jnp.bfloat16)

        @pl.when(g == 0)
        def _():
            for copy in weight_copies(2):
                copy.wait()

        acts = active[...]
        for start in range(0, width, 256):
            columns = pl.ds(start, 256)
            result = jnp.dot(acts, w_down[:, columns], preferred_element_type=jnp.float32)
            partial[g, :, :, columns] = result.astype(jnp.bfloat16).reshape(peers, rows, 256)
        pair_copy(g).start()

    def combine(g):
        pair_copy(g).wait_recv()
        for step in range(1, chips + 1):
            target = lax.rem(chip + step, chips)
            both = (partial[g, slot_of(target, core)].astype(jnp.float32)
                    + pair_in[g, target].astype(jnp.float32)).astype(jnp.bfloat16)
            pair_out[g, target] = both
            if step < chips:
                return_copy(g, step).start()

    def leave(g):
        total = x_in[g].astype(jnp.float32) + pair_out[g, chip].astype(jnp.float32)
        for step in range(1, chips):
            origin = lax.rem(chip + step, chips)
            return_arrival(g, origin).wait_recv()
            total += returned[g, origin].astype(jnp.float32)
        out[g] = total.astype(jnp.bfloat16)

        @pl.when(section < sections - 1)
        def _():
            pass_copy(g).start()

    for step in range(1, peers):
        share_copy(step).start()

    def one(g, carry):
        enter(g)
        forward(g)
        experts_block(g)
        combine(g)
        leave(g)
        return carry

    lax.fori_loop(0, groups, one, 0)

    for step in range(1, peers):
        share_copy(step).wait_send()

    def drain(g, carry):
        @pl.when(section > 0)
        def _():
            token_copy(g, section).wait_send()

        @pl.when(section < sections - 1)
        def _():
            pass_copy(g).wait_send()

        sibling_copy(g).wait_send()
        pair_copy(g).wait_send()
        for step in range(1, chips):
            gather_copy(g, step).wait_send()
            forward_copy(g, step).wait_send()
            return_copy(g, step).wait_send()
        return carry

    lax.fori_loop(0, groups, drain, 0)


def local(sections, peers, tokens, norm_gain, gate_weight, up_weight, down_weight, expert_ids,
          gate_probs):
    micro, rows_each, part = tokens.shape
    width = norm_gain.shape[1]
    groups, rows = micro // GROUP, rows_each * GROUP
    experts_local, ff = gate_weight.shape[1], gate_weight.shape[3]
    hidden = experts_local * ff
    top = expert_ids.shape[3]
    chips = peers // 2
    vmem = pl.BlockSpec(memory_space=pltpu.VMEM)
    anywhere = pl.BlockSpec(memory_space=pl.ANY)
    dma = pltpu.SemaphoreType.DMA
    bf16 = jnp.bfloat16
    result = pl.pallas_call(
        functools.partial(kernel, sections, peers, experts_local),
        out_shape=jax.ShapeDtypeStruct((groups, rows, width), bf16),
        in_specs=[vmem, vmem, anywhere, anywhere, anywhere, vmem, vmem],
        out_specs=vmem,
        scratch_shapes=[
            pltpu.VMEM((width, hidden), bf16),
            pltpu.VMEM((width, hidden), bf16),
            pltpu.VMEM((hidden, width), bf16),
            pltpu.VMEM((groups, rows, width), bf16),
            pltpu.VMEM((groups, peers, rows, width), bf16),
            pltpu.VMEM((peers * rows, hidden), bf16),
            pltpu.VMEM((groups, peers, rows, width), bf16),
            pltpu.VMEM((groups, chips, rows, width), bf16),
            pltpu.VMEM((groups, chips, rows, width), bf16),
            pltpu.VMEM((groups, chips, rows, width), bf16),
            pltpu.VMEM((peers, rows, LANES), jnp.float32),
            dma((3, experts_local)),
            dma((groups,)),
            dma((groups, sections)),
            dma((peers,)),
            dma((peers,)),
            dma((groups, chips)),
            dma((groups, peers)),
            dma((groups, chips)),
            dma((groups,)),
            dma((groups,)),
            dma((groups, chips)),
            dma((groups, chips)),
            dma((groups,)),
            dma((groups,)),
        ],
        compiler_params=pltpu.CompilerParams(
            collective_id=0, has_side_effects=True, vmem_limit_bytes=58 * 2**20
        ),
    )(
        tokens.reshape(groups, rows, part),
        norm_gain,
        gate_weight[0],
        up_weight[0],
        down_weight[0],
        expert_ids[0].reshape(groups, rows, top),
        gate_probs[0].reshape(groups, rows, top),
    )
    return result.reshape(1, micro, rows_each, width)


def solution(mesh):
    in_specs = (
        P(None, "expert", "section"),
        P("section", None),
        P("section", "expert", None, None),
        P("section", "expert", None, None),
        P("section", "expert", None, None),
        P("section", None, "expert", None),
        P("section", None, "expert", None),
    )
    out_specs = P("section", None, "expert", None)
    body = functools.partial(local, mesh.shape["section"], mesh.shape["expert"])
    return jax.shard_map(body, mesh=mesh, in_specs=in_specs, out_specs=out_specs, check_vma=False)
```

time: 483 us -> 119 us (0.25); the launches traced: 476 us -> 119 us
  waiting for transfers between devices: 174 us -> 0 us
  matrix products: 125 us -> 0 us
  Pallas kernels: 0 us -> 117 us
  starting transfers between devices: 89.6 us -> 0 us
  other arithmetic: 40.3 us -> 0 us
  local copies, waits for them, and re-layouts: 32.6 us -> 1.67 us
  blocking collectives: 14.7 us -> 0 us
    dot_general x44 -> x0, matrix products: 125 us -> none  [the longest x11 70.4 us: expert_block(): jnp.einsum('escf,efd->escd', active, w_down, preferred_element_type=jnp.f...]
    all_to_all x22 -> x0, waiting for transfers between devices: 124 us -> none  [the longest x11 66 us: moe_layer(): lax.all_to_all(results, 'expert', split_axis=1, concat_axis=0, tiled=True)]
    pallas_call x0 -> x1, Pallas kernels: none -> 117 us  [local(): pl.pallas_call(functools.partial(kernel, sections, peers, experts_local),...]
    all_to_all x22 -> x0, starting transfers between devices: 75.4 us -> none  [the longest x11 37.8 us: moe_layer(): lax.all_to_all(sending, 'expert', split_axis=0, concat_axis=1, tiled=True)]
    ppermute x11 -> x0, waiting for transfers between devices: 49.6 us -> none  [passed_along(): return lax.ppermute(value, axis, pairs)]
    all_gather x1 -> x0, blocking collectives: 14.7 us -> none  [local(): full_tokens = lax.all_gather(tokens, 'section', axis=2, tiled=True)]
    reduce_sum x55 -> x0, other arithmetic: 14.5 us -> none  [the longest x11 8.86 us: moe_layer(): weight = gate_share / jnp.sum(gate_share, axis=-1, keepdims=True)]
    ppermute x11 -> x0, starting transfers between devices: 14.2 us -> none  [passed_along(): return lax.ppermute(value, axis, pairs)]
  transfers between devices with their start and end apart: 33 -> 0, of which waited for: 33 -> 0; matrix products, arithmetic and copies ran while one was open for 6% -> 0% of each run, Pallas kernels for 0% -> 0%
where the time goes in v1:
time: 119 us
  Pallas kernels  117 us (98%)
  local copies, waits for them, and re-layouts  1.67 us (1%)
    pallas_call x1, Pallas kernels, local(): pl.pallas_call(functools.partial(kernel, sections, peers, experts_local),...  117 us

profile of v1, /device:TPU:24, one launch (start us, length us, event | category | flops | bytes accessed | tf_op | source)
XLA Modules:
  0.0 118.9 jit_solution(1849885370876916651)
XLA Ops:
  0.0 117.3 %shard_map.73 = bf16[4,16,2048]{2,1,0:T(8,128)(2,1)} custom-call(bf16[4,16,512]{2,1,0:T(8,128)(2,1)} %bitcast.11, f32[1,2048]{1,0:T(1,128)} %gain.1, bf16[4,2048,384]{2,1,0:T(8,128)(2,1)} %bitcast.7, bf16[4,2048,384]{2,1,0:T(8,128)(2,1)} %bitcast.8, bf16[4,384,2048]{2,1,0:T(8,128)(2,1)} %bitcast.9, s32[4,16,8]{2,1,0:T(8,128)} %bitcast.12, f32[4,16,8]{2,1,0:T(8,128)} %bitcast.13), custom_call_target="tpu_custom_call" | custom-call | tf_op jit(solution)/shard_map/pallas_call | solution.py:277
  117.3 1.7 %copy.9 = bf16[1,8,8,2048]{3,2,1,0:T(8,128)(2,1)} copy(bf16[1,8,8,2048]{3,2,1,0:T(8,128)(2,1)} %bitcast.10) | data formatting | bytes 524288

commit v2 on v1

--- a/solution.py
+++ b/solution.py
@@ -9,6 +9,7 @@
 
 EPS = 1e-06
 GROUP = 2
+HALVES = 2
 MESH = pl.DeviceIdType.MESH
 LANES = 128
 
@@ -118,22 +119,26 @@
         return remote(normed.at[g, slot], normed.at[g, slot], gather_send.at[g, 0],
                       gather_recv.at[g, slot], at_peer(sibling))
 
-    def pair_copy(g):
-        return remote(partial.at[g, pl.ds(other * chips, chips)], pair_in.at[g],
-                      pair_send.at[g], pair_recv.at[g], at_peer(sibling))
-
-    def return_copy(g, step):
+    half = width // HALVES
+
+    def pair_copy(g, h):
+        return remote(partial.at[g, h, pl.ds(other * chips, chips)], pair_in.at[g, h],
+                      pair_send.at[g, h], pair_recv.at[g, h], at_peer(sibling))
+
+    def return_copy(g, h, step):
         target = lax.rem(chip + step, chips)
-        return remote(pair_out.at[g, target], returned.at[g, chip], return_send.at[g, step],
-                      return_recv.at[g, chip], at_peer(target * 2 + core))
-
-    def return_arrival(g, origin):
-        return remote(pair_out.at[g, origin], returned.at[g, origin], return_send.at[g, 0],
-                      return_recv.at[g, origin], at_peer(sibling))
-
-    def pass_copy(g):
-        return remote(out.at[g], x_in.at[g], pass_send.at[g], pass_recv.at[g],
-                      at_section(lax.rem(section + 1, sections)))
+        return remote(pair_out.at[g, h, target], returned.at[g, h, chip],
+                      return_send.at[g, h, step], return_recv.at[g, h, chip],
+                      at_peer(target * 2 + core))
+
+    def return_arrival(g, h, origin):
+        return remote(pair_out.at[g, h, origin], returned.at[g, h, origin],
+                      return_send.at[g, h, 0], return_recv.at[g, h, origin], at_peer(sibling))
+
+    def pass_copy(g, h):
+        columns = pl.ds(h * half, half)
+        return remote(out.at[g, :, columns], x_in.at[g, :, columns], pass_send.at[g, h],
+                      pass_recv.at[g, h], at_section(lax.rem(section + 1, sections)))
 
     def enter(g):
         @pl.when(section == 0)
@@ -144,7 +149,8 @@
 
         @pl.when(section > 0)
         def _():
-            pass_copy(g).wait_recv()
+            for h in range(HALVES):
+                pass_copy(g, h).wait_recv()
 
         wide = x_in[g].astype(jnp.float32)
         scale = lax.rsqrt(jnp.mean(wide * wide, axis=-1, keepdims=True) + EPS)
@@ -162,7 +168,7 @@
     tile = 256 if hidden % 256 == 0 else LANES
     wide_lane = lax.broadcasted_iota(jnp.int32, (total_rows, LANES), 1)
 
-    def experts_block(g):
+    def project_in(g):
         for step in range(chips):
             gather_arrival(g, slot_of(lax.rem(chip + step, chips), other)).wait_recv()
 
@@ -183,6 +189,12 @@
             factor.append(jnp.sum(jnp.where(pick, every, 0.0), axis=-1, keepdims=True))
         rows_in = normed[g].reshape(total_rows, width)
         for start in range(0, hidden, tile):
+            if start == hidden // tile // 2 * tile:
+                @pl.when(g > 0)
+                def _():
+                    for h in range(HALVES):
+                        leave(g - 1, h)
+
             columns = pl.ds(start, tile)
             gate = jnp.dot(rows_in, w_gate[:, columns], preferred_element_type=jnp.float32)
             up = jnp.dot(rows_in, w_up[:, columns], preferred_element_type=jnp.float32)
@@ -191,52 +203,71 @@
                 piece = mid[:, begin:begin + LANES] * factor[(start + begin) // ff]
                 active[:, pl.ds(start + begin, LANES)] = piece.astype(jnp.bfloat16)
 
-        @pl.when(g == 0)
-        def _():
-            for copy in weight_copies(2):
-                copy.wait()
+    def project_out(g, h):
+        if h == 0:
+            @pl.when(g == 0)
+            def _():
+                for copy in weight_copies(2):
+                    copy.wait()
 
         acts = active[...]
-        for start in range(0, width, 256):
-            columns = pl.ds(start, 256)
+        for start in range(0, half, 256):
+            columns = pl.ds(h * half + start, 256)
             result = jnp.dot(acts, w_down[:, columns], preferred_element_type=jnp.float32)
-            partial[g, :, :, columns] = result.astype(jnp.bfloat16).reshape(peers, rows, 256)
-        pair_copy(g).start()
-
-    def combine(g):
-        pair_copy(g).wait_recv()
+            partial[g, h, :, :, pl.ds(start, 256)] = (
+                result.astype(jnp.bfloat16).reshape(peers, rows, 256))
+        pair_copy(g, h).start()
+
+    def combine(g, h):
+        pair_copy(g, h).wait_recv()
         for step in range(1, chips + 1):
             target = lax.rem(chip + step, chips)
-            both = (partial[g, slot_of(target, core)].astype(jnp.float32)
-                    + pair_in[g, target].astype(jnp.float32)).astype(jnp.bfloat16)
-            pair_out[g, target] = both
+            both = (partial[g, h, slot_of(target, core)].astype(jnp.float32)
+                    + pair_in[g, h, target].astype(jnp.float32)).astype(jnp.bfloat16)
+            pair_out[g, h, target] = both
             if step < chips:
-                return_copy(g, step).start()
-
-    def leave(g):
-        total = x_in[g].astype(jnp.float32) + pair_out[g, chip].astype(jnp.float32)
+                return_copy(g, h, step).start()
+
+    def leave(g, h):
+        columns = pl.ds(h * half, half)
+        total = x_in[g, :, columns].astype(jnp.float32) + pair_out[g, h, chip].astype(jnp.float32)
         for step in range(1, chips):
             origin = lax.rem(chip + step, chips)
-            return_arrival(g, origin).wait_recv()
-            total += returned[g, origin].astype(jnp.float32)
-        out[g] = total.astype(jnp.bfloat16)
+            return_arrival(g, h, origin).wait_recv()
+            total += returned[g, h, origin].astype(jnp.float32)
+        out[g, :, columns] = total.astype(jnp.bfloat16)
 
         @pl.when(section < sections - 1)
         def _():
-            pass_copy(g).start()
+            pass_copy(g, h).start()
 
     for step in range(1, peers):
         share_copy(step).start()
 
+    enter(0)
+    forward(0)
+
     def one(g, carry):
-        enter(g)
-        forward(g)
-        experts_block(g)
-        combine(g)
-        leave(g)
+        project_in(g)
+
+        @pl.when(g < groups - 1)
+        def _():
+            enter(g + 1)
+
+        for h in range(HALVES):
+            project_out(g, h)
+        for h in range(HALVES):
+            combine(g, h)
+
+        @pl.when(g < groups - 1)
+        def _():
+            forward(g + 1)
+
         return carry
 
     lax.fori_loop(0, groups, one, 0)
+    for h in range(HALVES):
+        leave(groups - 1, h)
 
     for step in range(1, peers):
         share_copy(step).wait_send()
@@ -248,14 +279,17 @@
 
         @pl.when(section < sections - 1)
         def _():
-            pass_copy(g).wait_send()
+            for h in range(HALVES):
+                pass_copy(g, h).wait_send()
 
         sibling_copy(g).wait_send()
-        pair_copy(g).wait_send()
         for step in range(1, chips):
             gather_copy(g, step).wait_send()
             forward_copy(g, step).wait_send()
-            return_copy(g, step).wait_send()
+        for h in range(HALVES):
+            pair_copy(g, h).wait_send()
+            for step in range(1, chips):
+                return_copy(g, h, step).wait_send()
         return carry
 
     lax.fori_loop(0, groups, drain, 0)
@@ -286,10 +320,10 @@
             pltpu.VMEM((groups, rows, width), bf16),
             pltpu.VMEM((groups, peers, rows, width), bf16),
             pltpu.VMEM((peers * rows, hidden), bf16),
-            pltpu.VMEM((groups, peers, rows, width), bf16),
-            pltpu.VMEM((groups, chips, rows, width), bf16),
-            pltpu.VMEM((groups, chips, rows, width), bf16),
-            pltpu.VMEM((groups, chips, rows, width), bf16),
+            pltpu.VMEM((groups, HALVES, peers, rows, width // HALVES), bf16),
+            pltpu.VMEM((groups, HALVES, chips, rows, width // HALVES), bf16),
+            pltpu.VMEM((groups, HALVES, chips, rows, width // HALVES), bf16),
+            pltpu.VMEM((groups, HALVES, chips, rows, width // HALVES), bf16),
             pltpu.VMEM((peers, rows, LANES), jnp.float32),
             dma((3, experts_local)),
             dma((groups,)),
@@ -299,12 +333,12 @@
             dma((groups, chips)),
             dma((groups, peers)),
             dma((groups, chips)),
-            dma((groups,)),
-            dma((groups,)),
-            dma((groups, chips)),
-            dma((groups, chips)),
-            dma((groups,)),
-            dma((groups,)),
+            dma((groups, HALVES)),
+            dma((groups, HALVES)),
+            dma((groups, HALVES, chips)),
+            dma((groups, HALVES, chips)),
+            dma((groups, HALVES)),
+            dma((groups, HALVES)),
         ],
         compiler_params=pltpu.CompilerParams(
             collective_id=0, has_side_effects=True, vmem_limit_bytes=58 * 2**20

time: 119 us -> 114 us (0.958)
  Pallas kernels: 117 us -> 112 us
    pallas_call x1, Pallas kernels: 117 us -> 112 us  [local(): pl.pallas_call(functools.partial(kernel, sections, peers, experts_local),...]
where the time goes in v2:
time: 114 us
  Pallas kernels  112 us (98%)
  local copies, waits for them, and re-layouts  1.67 us (1%)
    pallas_call x1, Pallas kernels, local(): pl.pallas_call(functools.partial(kernel, sections, peers, experts_local),...  112 us

profile of v2, /device:TPU:24, one launch (start us, length us, event | category | flops | bytes accessed | tf_op | source)
XLA Modules:
  0.0 114.0 jit_solution(5618236268529447479)
XLA Ops:
  0.0 112.4 %shard_map.73 = bf16[4,16,2048]{2,1,0:T(8,128)(2,1)} custom-call(bf16[4,16,512]{2,1,0:T(8,128)(2,1)} %bitcast.11, f32[1,2048]{1,0:T(1,128)} %gain.1, bf16[4,2048,384]{2,1,0:T(8,128)(2,1)} %bitcast.7, bf16[4,2048,384]{2,1,0:T(8,128)(2,1)} %bitcast.8, bf16[4,384,2048]{2,1,0:T(8,128)(2,1)} %bitcast.9, s32[4,16,8]{2,1,0:T(8,128)} %bitcast.12, f32[4,16,8]{2,1,0:T(8,128)} %bitcast.13), custom_call_target="tpu_custom_call" | custom-call | tf_op jit(solution)/shard_map/pallas_call | solution.py:311
  112.4 1.7 %copy.9 = bf16[1,8,8,2048]{3,2,1,0:T(8,128)(2,1)} copy(bf16[1,8,8,2048]{3,2,1,0:T(8,128)(2,1)} %bitcast.10) | data formatting | bytes 524288

commit v3 on v2

--- a/solution.py
+++ b/solution.py
@@ -165,7 +165,7 @@
             forward_copy(g, step).start()
 
     total_rows = peers * rows
-    tile = 256 if hidden % 256 == 0 else LANES
+    tile = 512 if hidden % 512 == 0 else hidden
     wide_lane = lax.broadcasted_iota(jnp.int32, (total_rows, LANES), 1)
 
     def project_in(g):
@@ -211,11 +211,9 @@
                     copy.wait()
 
         acts = active[...]
-        for start in range(0, half, 256):
-            columns = pl.ds(h * half + start, 256)
-            result = jnp.dot(acts, w_down[:, columns], preferred_element_type=jnp.float32)
-            partial[g, h, :, :, pl.ds(start, 256)] = (
-                result.astype(jnp.bfloat16).reshape(peers, rows, 256))
+        result = jnp.dot(acts, w_down[:, pl.ds(h * half, half)],
+                         preferred_element_type=jnp.float32)
+        partial[g, h] = result.astype(jnp.bfloat16).reshape(peers, rows, half)
         pair_copy(g, h).start()
 
     def combine(g, h):

time: 114 us -> 115 us (level)
  no operation moved by 1% of the time
where the time goes in v3:
time: 115 us
  Pallas kernels  113 us (98%)
  local copies, waits for them, and re-layouts  1.67 us (1%)
    pallas_call x1, Pallas kernels, local(): pl.pallas_call(functools.partial(kernel, sections, peers, experts_local),...  113 us

profile of v3, /device:TPU:24, one launch (start us, length us, event | category | flops | bytes accessed | tf_op | source)
XLA Modules:
  0.0 114.6 jit_solution(7530999737045753305)
XLA Ops:
  0.0 112.9 %shard_map.73 = bf16[4,16,2048]{2,1,0:T(8,128)(2,1)} custom-call(bf16[4,16,512]{2,1,0:T(8,128)(2,1)} %bitcast.11, f32[1,2048]{1,0:T(1,128)} %gain.1, bf16[4,2048,384]{2,1,0:T(8,128)(2,1)} %bitcast.7, bf16[4,2048,384]{2,1,0:T(8,128)(2,1)} %bitcast.8, bf16[4,384,2048]{2,1,0:T(8,128)(2,1)} %bitcast.9, s32[4,16,8]{2,1,0:T(8,128)} %bitcast.12, f32[4,16,8]{2,1,0:T(8,128)} %bitcast.13), custom_call_target="tpu_custom_call" | custom-call | tf_op jit(solution)/shard_map/pallas_call | solution.py:309
  113.0 1.7 %copy.9 = bf16[1,8,8,2048]{3,2,1,0:T(8,128)(2,1)} copy(bf16[1,8,8,2048]{3,2,1,0:T(8,128)(2,1)} %bitcast.10) | data formatting | bytes 524288

commit v4 on v3

--- a/solution.py
+++ b/solution.py
@@ -243,23 +243,31 @@
         share_copy(step).start()
 
     enter(0)
+    ahead = jnp.where(section == 0, 2, 1)
+
+    @pl.when(section == 0)
+    def _():
+        enter(1)
+
     forward(0)
 
     def one(g, carry):
         project_in(g)
 
-        @pl.when(g < groups - 1)
-        def _():
-            enter(g + 1)
+        @pl.when(g + ahead < groups)
+        def _():
+            enter(g + ahead)
 
         for h in range(HALVES):
             project_out(g, h)
-        for h in range(HALVES):
+        for h in range(HALVES - 1):
             combine(g, h)
 
         @pl.when(g < groups - 1)
         def _():
             forward(g + 1)
+
+        combine(g, HALVES - 1)
 
         return carry
 

time: 115 us -> 116 us (level)
  no operation moved by 1% of the time
where the time goes in v4:
time: 116 us; the launch traced here: 115 us
  Pallas kernels  114 us (98%)
  local copies, waits for them, and re-layouts  1.67 us (1%)
    pallas_call x1, Pallas kernels, local(): pl.pallas_call(functools.partial(kernel, sections, peers, experts_local),...  114 us

profile of v4, /device:TPU:24, one launch (start us, length us, event | category | flops | bytes accessed | tf_op | source)
XLA Modules:
  0.0 115.2 jit_solution(6774973214804445251)
XLA Ops:
  0.0 113.6 %shard_map.73 = bf16[4,16,2048]{2,1,0:T(8,128)(2,1)} custom-call(bf16[4,16,512]{2,1,0:T(8,128)(2,1)} %bitcast.11, f32[1,2048]{1,0:T(1,128)} %gain.1, bf16[4,2048,384]{2,1,0:T(8,128)(2,1)} %bitcast.7, bf16[4,2048,384]{2,1,0:T(8,128)(2,1)} %bitcast.8, bf16[4,384,2048]{2,1,0:T(8,128)(2,1)} %bitcast.9, s32[4,16,8]{2,1,0:T(8,128)} %bitcast.12, f32[4,16,8]{2,1,0:T(8,128)} %bitcast.13), custom_call_target="tpu_custom_call" | custom-call | tf_op jit(solution)/shard_map/pallas_call | solution.py:317
  113.6 1.7 %copy.9 = bf16[1,8,8,2048]{3,2,1,0:T(8,128)(2,1)} copy(bf16[1,8,8,2048]{3,2,1,0:T(8,128)(2,1)} %bitcast.10) | data formatting | bytes 524288

commit v5 on v4

--- a/solution.py
+++ b/solution.py
@@ -8,7 +8,7 @@
 from jax.sharding import PartitionSpec as P
 
 EPS = 1e-06
-GROUP = 2
+GROUP = 4
 HALVES = 2
 MESH = pl.DeviceIdType.MESH
 LANES = 128

time: 116 us -> 136 us (1.17)
  Pallas kernels: 114 us -> 134 us
    pallas_call x1, Pallas kernels: 114 us -> 134 us  [local(): pl.pallas_call(functools.partial(kernel, sections, peers, experts_local),...]
where the time goes in v5:
time: 136 us
  Pallas kernels  134 us (99%)
  local copies, waits for them, and re-layouts  1.67 us (1%)
    pallas_call x1, Pallas kernels, local(): pl.pallas_call(functools.partial(kernel, sections, peers, experts_local),...  134 us

profile of v5, /device:TPU:24, one launch (start us, length us, event | category | flops | bytes accessed | tf_op | source)
XLA Modules:
  0.0 135.8 jit_solution(6957848689613707352)
XLA Ops:
  0.0 134.1 %shard_map.73 = bf16[2,32,2048]{2,1,0:T(8,128)(2,1)} custom-call(bf16[2,32,512]{2,1,0:T(8,128)(2,1)} %bitcast.11, f32[1,2048]{1,0:T(1,128)} %gain.1, bf16[4,2048,384]{2,1,0:T(8,128)(2,1)} %bitcast.7, bf16[4,2048,384]{2,1,0:T(8,128)(2,1)} %bitcast.8, bf16[4,384,2048]{2,1,0:T(8,128)(2,1)} %bitcast.9, s32[2,32,8]{2,1,0:T(8,128)} %bitcast.12, f32[2,32,8]{2,1,0:T(8,128)} %bitcast.13), custom_call_target="tpu_custom_call" | custom-call | tf_op jit(solution)/shard_map/pallas_call | solution.py:317
  134.1 1.7 %copy.9 = bf16[1,8,8,2048]{3,2,1,0:T(8,128)(2,1)} copy(bf16[1,8,8,2048]{3,2,1,0:T(8,128)(2,1)} %bitcast.10) | data formatting | bytes 524288

commit v6 on v4

--- a/solution.py
+++ b/solution.py
@@ -9,6 +9,8 @@
 
 EPS = 1e-06
 GROUP = 2
+CAP = 2
+BLOCK = 8
 HALVES = 2
 MESH = pl.DeviceIdType.MESH
 LANES = 128
@@ -18,7 +20,7 @@
     sections, peers, experts_local,
     tokens, gain, gate_hbm, up_hbm, down_hbm, ids, probs,
     out,
-    w_gate, w_up, w_down, x_in, normed, active, partial, pair_in, pair_out, returned, shares,
+    w_in, w_down, x_in, normed, active, chosen, partial, pair_in, pair_out, returned, shares,
     weight_sem, token_send, token_recv, share_send, share_recv, gather_send, gather_recv,
     forward_send, pair_send, pair_recv, return_send, return_recv, pass_send, pass_recv,
 ):
@@ -42,14 +44,14 @@
     def weight_copies(which):
         copies = []
         for e in range(experts_local):
-            span = pl.ds(e * ff, ff)
             if which < 2:
-                source, target = ((gate_hbm, w_gate), (up_hbm, w_up))[which]
+                source = (gate_hbm, up_hbm)[which]
                 copies.append(pltpu.make_async_copy(
-                    source.at[e], target.at[:, span], weight_sem.at[which, e]))
+                    source.at[e], w_in.at[:, pl.ds((2 * e + which) * ff, ff)],
+                    weight_sem.at[which, e]))
             else:
                 copies.append(pltpu.make_async_copy(
-                    down_hbm.at[e], w_down.at[span], weight_sem.at[which, e]))
+                    down_hbm.at[e], w_down.at[pl.ds(e * ff, ff)], weight_sem.at[which, e]))
         return copies
 
     for copy in weight_copies(0) + weight_copies(1) + weight_copies(2):
@@ -165,17 +167,14 @@
             forward_copy(g, step).start()
 
     total_rows = peers * rows
-    tile = 512 if hidden % 512 == 0 else hidden
+    slots = CAP * (total_rows // BLOCK)
+    all_slots = experts_local * slots
     wide_lane = lax.broadcasted_iota(jnp.int32, (total_rows, LANES), 1)
+    slot_lane = lax.broadcasted_iota(jnp.int32, (total_rows, all_slots), 1).astype(jnp.float32)
 
     def project_in(g):
-        for step in range(chips):
-            gather_arrival(g, slot_of(lax.rem(chip + step, chips), other)).wait_recv()
-
         @pl.when(g == 0)
         def _():
-            for copy in weight_copies(0) + weight_copies(1):
-                copy.wait()
             for step in range(1, peers):
                 origin = lax.rem(index + step, peers)
                 slot = slot_of(lax.div(origin, 2), lax.rem(origin, 2))
@@ -183,25 +182,46 @@
                        share_recv.at[slot], at_peer(origin)).wait_recv()
 
         every = shares[...].reshape(total_rows, LANES)
-        factor = []
+        below = (lax.broadcasted_iota(jnp.int32, (total_rows, total_rows), 0)
+                 > lax.broadcasted_iota(jnp.int32, (total_rows, total_rows), 1))
+        ranks = jnp.dot(jnp.where(below, 1.0, 0.0).astype(jnp.bfloat16),
+                        jnp.where(every > 0.0, 1.0, 0.0).astype(jnp.bfloat16),
+                        preferred_element_type=jnp.float32)
+        weighted = jnp.zeros((total_rows, all_slots), jnp.float32)
         for e in range(experts_local):
             pick = wide_lane == g * experts + index * experts_local + e
-            factor.append(jnp.sum(jnp.where(pick, every, 0.0), axis=-1, keepdims=True))
-        rows_in = normed[g].reshape(total_rows, width)
-        for start in range(0, hidden, tile):
-            if start == hidden // tile // 2 * tile:
+            factor = jnp.sum(jnp.where(pick, every, 0.0), axis=-1, keepdims=True)
+            rank = jnp.sum(jnp.where(pick, ranks, 0.0), axis=-1, keepdims=True)
+            inside = (slot_lane >= e * slots) & (slot_lane < (e + 1) * slots)
+            weighted += jnp.where(inside & (rank + e * slots == slot_lane), factor, 0.0)
+        chosen[...] = jnp.where(weighted > 0.0, 1.0, 0.0).astype(jnp.bfloat16)
+        flipped = weighted.T
+        slot_share = jnp.sum(flipped, axis=-1, keepdims=True)
+        picker = jnp.where(flipped > 0.0, 1.0, 0.0).astype(jnp.bfloat16)
+
+        for step in range(chips):
+            gather_arrival(g, slot_of(lax.rem(chip + step, chips), other)).wait_recv()
+
+        @pl.when(g == 0)
+        def _():
+            for copy in weight_copies(0) + weight_copies(1):
+                copy.wait()
+
+        rows_in = jnp.dot(picker, normed[g].reshape(total_rows, width),
+                          preferred_element_type=jnp.float32).astype(jnp.bfloat16)
+        for e in range(experts_local):
+            if e == experts_local // 2:
                 @pl.when(g > 0)
                 def _():
                     for h in range(HALVES):
                         leave(g - 1, h)
 
-            columns = pl.ds(start, tile)
-            gate = jnp.dot(rows_in, w_gate[:, columns], preferred_element_type=jnp.float32)
-            up = jnp.dot(rows_in, w_up[:, columns], preferred_element_type=jnp.float32)
-            mid = gate / (1.0 + jnp.exp(-gate)) * up
-            for begin in range(0, tile, LANES):
-                piece = mid[:, begin:begin + LANES] * factor[(start + begin) // ff]
-                active[:, pl.ds(start + begin, LANES)] = piece.astype(jnp.bfloat16)
+            span = slice(e * slots, (e + 1) * slots)
+            both = jnp.dot(rows_in[span], w_in[:, pl.ds(2 * e * ff, 2 * ff)],
+                           preferred_element_type=jnp.float32)
+            gate, up = both[:, :ff], both[:, ff:]
+            mid = gate / (1.0 + jnp.exp(-gate)) * up * slot_share[span]
+            active[e] = mid.astype(jnp.bfloat16)
 
     def project_out(g, h):
         if h == 0:
@@ -210,8 +230,13 @@
                 for copy in weight_copies(2):
                     copy.wait()
 
-        acts = active[...]
-        result = jnp.dot(acts, w_down[:, pl.ds(h * half, half)],
+        columns = pl.ds(h * half, half)
+        pieces = [
+            jnp.dot(active[e], w_down[pl.ds(e * ff, ff), columns],
+                    preferred_element_type=jnp.float32).astype(jnp.bfloat16)
+            for e in range(experts_local)
+        ]
+        result = jnp.dot(chosen[...], jnp.concatenate(pieces, axis=0),
                          preferred_element_type=jnp.float32)
         partial[g, h] = result.astype(jnp.bfloat16).reshape(peers, rows, half)
         pair_copy(g, h).start()
@@ -310,6 +335,7 @@
     hidden = experts_local * ff
     top = expert_ids.shape[3]
     chips = peers // 2
+    slots = CAP * (peers * rows // BLOCK)
     vmem = pl.BlockSpec(memory_space=pltpu.VMEM)
     anywhere = pl.BlockSpec(memory_space=pl.ANY)
     dma = pltpu.SemaphoreType.DMA
@@ -320,12 +346,12 @@
         in_specs=[vmem, vmem, anywhere, anywhere, anywhere, vmem, vmem],
         out_specs=vmem,
         scratch_shapes=[
-            pltpu.VMEM((width, hidden), bf16),
-            pltpu.VMEM((width, hidden), bf16),
+            pltpu.VMEM((width, 2 * hidden), bf16),
             pltpu.VMEM((hidden, width), bf16),
             pltpu.VMEM((groups, rows, width), bf16),
             pltpu.VMEM((groups, peers, rows, width), bf16),
-            pltpu.VMEM((peers * rows, hidden), bf16),
+            pltpu.VMEM((experts_local, slots, ff), bf16),
+            pltpu.VMEM((peers * rows, experts_local * slots), bf16),
             pltpu.VMEM((groups, HALVES, peers, rows, width // HALVES), bf16),
             pltpu.VMEM((groups, HALVES, chips, rows, width // HALVES), bf16),
             pltpu.VMEM((groups, HALVES, chips, rows, width // HALVES), bf16),

time: 116 us -> 116 us (level)
  no operation moved by 1% of the time
where the time goes in v6:
time: 116 us
  Pallas kernels  114 us (98%)
  local copies, waits for them, and re-layouts  1.67 us (1%)
    pallas_call x1, Pallas kernels, local(): pl.pallas_call(functools.partial(kernel, sections, peers, experts_local),...  114 us

profile of v6, /device:TPU:24, one launch (start us, length us, event | category | flops | bytes accessed | tf_op | source)
XLA Modules:
  0.0 115.7 jit_solution(9209449811419140342)
XLA Ops:
  0.0 114.0 %shard_map.73 = bf16[4,16,2048]{2,1,0:T(8,128)(2,1)} custom-call(bf16[4,16,512]{2,1,0:T(8,128)(2,1)} %bitcast.11, f32[1,2048]{1,0:T(1,128)} %gain.1, bf16[4,2048,384]{2,1,0:T(8,128)(2,1)} %bitcast.7, bf16[4,2048,384]{2,1,0:T(8,128)(2,1)} %bitcast.8, bf16[4,384,2048]{2,1,0:T(8,128)(2,1)} %bitcast.9, s32[4,16,8]{2,1,0:T(8,128)} %bitcast.12, f32[4,16,8]{2,1,0:T(8,128)} %bitcast.13), custom_call_target="tpu_custom_call" | custom-call | tf_op jit(solution)/shard_map/pallas_call | solution.py:343
  114.0 1.7 %copy.9 = bf16[1,8,8,2048]{3,2,1,0:T(8,128)(2,1)} copy(bf16[1,8,8,2048]{3,2,1,0:T(8,128)(2,1)} %bitcast.10) | data formatting | bytes 524288

commit v7 on v6

--- a/solution.py
+++ b/solution.py
@@ -210,12 +210,6 @@
         rows_in = jnp.dot(picker, normed[g].reshape(total_rows, width),
                           preferred_element_type=jnp.float32).astype(jnp.bfloat16)
         for e in range(experts_local):
-            if e == experts_local // 2:
-                @pl.when(g > 0)
-                def _():
-                    for h in range(HALVES):
-                        leave(g - 1, h)
-
             span = slice(e * slots, (e + 1) * slots)
             both = jnp.dot(rows_in[span], w_in[:, pl.ds(2 * e * ff, 2 * ff)],
                            preferred_element_type=jnp.float32)
@@ -285,6 +279,11 @@
 
         for h in range(HALVES):
             project_out(g, h)
+        @pl.when(g > 0)
+        def _():
+            for h in range(HALVES):
+                leave(g - 1, h)
+
         for h in range(HALVES - 1):
             combine(g, h)
 

time: 116 us -> 122 us (1.052)
  Pallas kernels: 114 us -> 120 us
    pallas_call x1, Pallas kernels: 114 us -> 120 us  [local(): pl.pallas_call(functools.partial(kernel, sections, peers, experts_local),...]
where the time goes in v7:
time: 122 us; the launch traced here: 121 us
  Pallas kernels  120 us (98%)
  local copies, waits for them, and re-layouts  1.67 us (1%)
    pallas_call x1, Pallas kernels, local(): pl.pallas_call(functools.partial(kernel, sections, peers, experts_local),...  120 us

profile of v7, /device:TPU:24, one launch (start us, length us, event | category | flops | bytes accessed | tf_op | source)
XLA Modules:
  0.0 121.4 jit_solution(1217408172240342855)
XLA Ops:
  0.0 119.7 %shard_map.73 = bf16[4,16,2048]{2,1,0:T(8,128)(2,1)} custom-call(bf16[4,16,512]{2,1,0:T(8,128)(2,1)} %bitcast.11, f32[1,2048]{1,0:T(1,128)} %gain.1, bf16[4,2048,384]{2,1,0:T(8,128)(2,1)} %bitcast.7, bf16[4,2048,384]{2,1,0:T(8,128)(2,1)} %bitcast.8, bf16[4,384,2048]{2,1,0:T(8,128)(2,1)} %bitcast.9, s32[4,16,8]{2,1,0:T(8,128)} %bitcast.12, f32[4,16,8]{2,1,0:T(8,128)} %bitcast.13), custom_call_target="tpu_custom_call" | custom-call | tf_op jit(solution)/shard_map/pallas_call | solution.py:342
  119.7 1.7 %copy.9 = bf16[1,8,8,2048]{3,2,1,0:T(8,128)(2,1)} copy(bf16[1,8,8,2048]{3,2,1,0:T(8,128)(2,1)} %bitcast.10) | data formatting | bytes 524288
